TPU v7x, 32 devices: a whole 2x2x4 slice. The times are simulated.
32 devices in a mesh: dp: 16 (over z, y, x), tensor: 2 (over core).
Axes of the slice: x: 2, y: 2, z: 4, core: 2. Of those that a mesh axis runs over, the one named last changes fastest.
Arguments:
- tokens: bfloat16 [32768, 768], P('dp'), may hold values from -6 to 6
- cotangent: bfloat16 [32768, 768], P('dp'), may hold values from -6 to 6
- long_lengths: int32 [32], P('dp'), may hold values from 129 to 512, as said below
- short_lengths: int32 [128], P('dp'), may hold values from 1 to 128, as said below
- live_counts: int32 [16, 2], P('dp'), may hold values from 1 to 8, as said below
- query_weight: bfloat16 [768, 768], P(None, 'tensor'), may hold values from -0.21875 to 0.21875
- query_bias: float32 [768], P('tensor'), may hold values from -3 to 3
- key_weight: bfloat16 [768, 768], P(None, 'tensor'), may hold values from -0.21875 to 0.21875
- value_weight: bfloat16 [768, 768], P(None, 'tensor'), may hold values from -0.21875 to 0.21875
- value_bias: float32 [768], P('tensor'), may hold values from -3 to 3
- output_weight: bfloat16 [768, 768], P('tensor'), may hold values from -3.5 to 3.5
- output_bias: float32 [768], replicated, may hold values from -3 to 3
- attn_gain: float32 [768], replicated, may hold values from 0.1 to 1.9
- attn_shift: float32 [768], replicated, may hold values from -3 to 3
- inner_weight: bfloat16 [768, 3072], P(None, 'tensor'), may hold values from -0.21875 to 0.21875
- inner_bias: float32 [3072], P('tensor'), may hold values from -3 to 3
- outer_weight: bfloat16 [3072, 768], P('tensor'), may hold values from -0.109375 to 0.109375
- outer_bias: float32 [768], replicated, may hold values from -3 to 3
- ffn_gain: float32 [768], replicated, may hold values from 0.1 to 1.9
- ffn_shift: float32 [768], replicated, may hold values from -3 to 3
Outputs:
- result: bfloat16 [32768, 768], P('dp')
- pooled: float32 [160, 768], P('dp')
- input_grad: float32 [32768, 768], P('dp')
- query_weight_grad: float32 [768, 768], P('dp', 'tensor')
- query_bias_grad: float32 [768], P('tensor')
- key_weight_grad: float32 [768, 768], P('dp', 'tensor')
- value_weight_grad: float32 [768, 768], P('dp', 'tensor')
- value_bias_grad: float32 [768], P('tensor')
- output_weight_grad: float32 [768, 768], P('tensor', 'dp')
- output_bias_grad: float32 [768], P('dp')
- attn_gain_grad: float32 [768], P('dp')
- attn_shift_grad: float32 [768], P('dp')
- inner_weight_grad: float32 [768, 3072], P('dp', 'tensor')
- inner_bias_grad: float32 [3072], P('tensor')
- outer_weight_grad: float32 [3072, 768], P('tensor', 'dp')
- outer_bias_grad: float32 [768], P('dp')
- ffn_gain_grad: float32 [768], P('dp')
- ffn_shift_grad: float32 [768], P('dp')
Inputs may be any that keep to these rules, and one draw needn't show every extreme that they name: `long_lengths`: each long slot's length is over 128; slot 0 of some device has exactly 512. `short_lengths`: slot 0 of some device has exactly 128. `live_counts`: row i gives device i's live long slots (column 0, at most 2) and live short slots (column 1, at most 8); the slots below a count are live; some device has all its slots live.
All inputs are finite; a program needn't handle non-finite values.
Results may differ from a plain program's by a relative error of at most 0.02.
Values may be sent and summed in bfloat16 or wider, within the bound.
A program may use at most 192 MiB of HBM per device.

v0:
```python
import jax
import jax.numpy as jnp
from jax import lax
from jax.sharding import PartitionSpec as P

HEAD_DIM = 64
LONG = 512
SHORT = 128
NL = 2
NS = 8


NORM_EPS = 1e-12
MASKED = -1000000000.0
SCORE_SCALE = 0.125
ROOT_HALF = 0.7071067811865476
INV_ROOT_TAU = 0.3989422804014327


def normalize(values, norm_gain, norm_shift):
    centre = values - jnp.mean(values, axis=-1, keepdims=True)
    inverse = lax.rsqrt(jnp.mean(centre * centre, axis=-1, keepdims=True) + NORM_EPS)
    normed = centre * inverse
    return (normed * norm_gain + norm_shift, normed, inverse)


def normalize_back(upstream, normed, inverse, norm_gain):
    scaled = upstream * norm_gain
    plain_mean = jnp.mean(scaled, axis=-1, keepdims=True)
    cross_mean = jnp.mean(scaled * normed, axis=-1, keepdims=True)
    value_grad = inverse * (scaled - plain_mean - normed * cross_mean)
    return (value_grad, jnp.sum(upstream * normed, axis=0), jnp.sum(upstream, axis=0))


def split_heads(row_values):
    long_part = row_values[: NL * LONG].reshape(NL, LONG, -1, HEAD_DIM)
    short_part = row_values[NL * LONG :].reshape(NS, SHORT, -1, HEAD_DIM)
    return (long_part, short_part)


def join_heads(long_part, short_part):
    return jnp.concatenate(
        [long_part.reshape(NL * LONG, -1), short_part.reshape(NS * SHORT, -1)], axis=0
    )


def masked_scores(queries, keys_in, key_valid):
    scores = (
        jnp.einsum("bqhd,bkhd->bhqk", queries, keys_in, preferred_element_type=jnp.float32)
        * SCORE_SCALE
    )
    return jnp.where(key_valid[:, None, None, :], scores, MASKED)


def attend_bucket(queries, keys_in, values_in, key_valid):
    scores = masked_scores(queries, keys_in, key_valid)
    highest = jnp.max(scores, axis=-1, keepdims=True)
    totals = jnp.sum(jnp.exp(scores - highest), axis=-1, keepdims=True)
    probs_low = (jnp.exp(scores - highest) / totals).astype(jnp.bfloat16)
    mixed_heads = jnp.einsum(
        "bhqk,bkhd->bqhd", probs_low, values_in, preferred_element_type=jnp.float32
    )
    return (mixed_heads, highest, totals)


def attend_back(queries, keys_in, values_in, key_valid, highest, totals, upstream):
    probs_full = jnp.exp(masked_scores(queries, keys_in, key_valid) - highest) / totals
    probs_low = probs_full.astype(jnp.bfloat16)
    prob_grad = jnp.einsum(
        "bqhd,bkhd->bhqk", upstream, values_in, preferred_element_type=jnp.float32
    )
    value_grad = jnp.einsum(
        "bhqk,bqhd->bkhd", probs_low, upstream, preferred_element_type=jnp.float32
    )
    row_delta = jnp.sum(prob_grad * probs_full, axis=-1, keepdims=True)
    score_grad = jnp.where(
        key_valid[:, None, None, :], probs_full * (prob_grad - row_delta), 0.0
    ).astype(jnp.bfloat16)
    query_grad = (
        jnp.einsum("bhqk,bkhd->bqhd", score_grad, keys_in, preferred_element_type=jnp.float32)
        * SCORE_SCALE
    )
    key_grad = (
        jnp.einsum("bhqk,bqhd->bkhd", score_grad, queries, preferred_element_type=jnp.float32)
        * SCORE_SCALE
    )
    return (query_grad, key_grad, value_grad)


def pool_rows(row_values, key_valid, lengths):
    sums = jnp.sum(row_values * key_valid[:, :, None].astype(jnp.float32), axis=1)
    return sums / jnp.maximum(lengths, 1).astype(jnp.float32)[:, None]


def per_device(
    tokens,
    cotangent,
    long_lengths,
    short_lengths,
    live_counts,
    query_weight,
    query_bias,
    key_weight,
    value_weight,
    value_bias,
    output_weight,
    output_bias,
    attn_gain,
    attn_shift,
    inner_weight,
    inner_bias,
    outer_weight,
    outer_bias,
    ffn_gain,
    ffn_shift,
):
    long_live = jnp.where(jnp.arange(NL) < live_counts[0, 0], long_lengths, 0)
    short_live = jnp.where(jnp.arange(NS) < live_counts[0, 1], short_lengths, 0)
    long_valid = jnp.arange(LONG)[None, :] < long_live[:, None]
    short_valid = jnp.arange(SHORT)[None, :] < short_live[:, None]
    queries = (
        jnp.dot(tokens, query_weight, preferred_element_type=jnp.float32) + query_bias
    ).astype(jnp.bfloat16)
    keys_low = jnp.dot(tokens, key_weight, preferred_element_type=jnp.float32).astype(jnp.bfloat16)
    values_low = (
        jnp.dot(tokens, value_weight, preferred_element_type=jnp.float32) + value_bias
    ).astype(jnp.bfloat16)
    long_query, short_query = split_heads(queries)
    long_keys, short_keys = split_heads(keys_low)
    long_values, short_values = split_heads(values_low)
    long_mixed, long_high, long_total = attend_bucket(
        long_query, long_keys, long_values, long_valid
    )
    short_mixed, short_high, short_total = attend_bucket(
        short_query, short_keys, short_values, short_valid
    )
    heads_low = join_heads(long_mixed, short_mixed).astype(jnp.bfloat16)
    attn_out = (
        lax.psum(
            jnp.dot(heads_low, output_weight, preferred_element_type=jnp.float32).astype(
                jnp.bfloat16
            ),
            "tensor",
        ).astype(jnp.float32)
        + output_bias
    )
    hidden_one, normed_one, inverse_one = normalize(
        tokens.astype(jnp.float32) + attn_out, attn_gain, attn_shift
    )
    hidden_low = hidden_one.astype(jnp.bfloat16)
    inner_pre = jnp.dot(hidden_low, inner_weight, preferred_element_type=jnp.float32) + inner_bias
    erf_part = lax.erf(inner_pre * ROOT_HALF)
    act_low = (0.5 * inner_pre * (1.0 + erf_part)).astype(jnp.bfloat16)
    ffn_out = (
        lax.psum(
            jnp.dot(act_low, outer_weight, preferred_element_type=jnp.float32).astype(jnp.bfloat16),
            "tensor",
        ).astype(jnp.float32)
        + outer_bias
    )
    output_full, normed_two, inverse_two = normalize(hidden_one + ffn_out, ffn_gain, ffn_shift)
    result = output_full.astype(jnp.bfloat16)
    pooled = jnp.concatenate(
        [
            pool_rows(output_full[: NL * LONG].reshape(NL, LONG, -1), long_valid, long_live),
            pool_rows(output_full[NL * LONG :].reshape(NS, SHORT, -1), short_valid, short_live),
        ],
        axis=0,
    )
    upstream = cotangent.astype(jnp.float32)
    resid_two_grad, ffn_gain_grad, ffn_shift_grad = normalize_back(
        upstream, normed_two, inverse_two, ffn_gain
    )
    branch_grad = resid_two_grad.astype(jnp.bfloat16)
    outer_bias_grad = jnp.sum(branch_grad.astype(jnp.float32), axis=0)
    outer_weight_grad = jnp.dot(act_low.T, branch_grad, preferred_element_type=jnp.float32)
    act_grad = jnp.dot(branch_grad, outer_weight.T, preferred_element_type=jnp.float32)
    gelu_slope = (
        0.5 * (1.0 + erf_part) + inner_pre * jnp.exp(-0.5 * inner_pre * inner_pre) * INV_ROOT_TAU
    )
    inner_grad = (act_grad * gelu_slope).astype(jnp.bfloat16)
    inner_bias_grad = jnp.sum(inner_grad.astype(jnp.float32), axis=0)
    inner_weight_grad = jnp.dot(hidden_low.T, inner_grad, preferred_element_type=jnp.float32)
    hidden_grad = (
        lax.psum(
            jnp.dot(inner_grad, inner_weight.T, preferred_element_type=jnp.float32).astype(
                jnp.bfloat16
            ),
            "tensor",
        ).astype(jnp.float32)
        + resid_two_grad
    )
    resid_one_grad, attn_gain_grad, attn_shift_grad = normalize_back(
        hidden_grad, normed_one, inverse_one, attn_gain
    )
    attn_grad = resid_one_grad.astype(jnp.bfloat16)
    output_bias_grad = jnp.sum(attn_grad.astype(jnp.float32), axis=0)
    output_weight_grad = jnp.dot(heads_low.T, attn_grad, preferred_element_type=jnp.float32)
    heads_grad = jnp.dot(attn_grad, output_weight.T, preferred_element_type=jnp.float32).astype(
        jnp.bfloat16
    )
    long_up, short_up = split_heads(heads_grad)
    long_grads = attend_back(
        long_query, long_keys, long_values, long_valid, long_high, long_total, long_up
    )
    short_grads = attend_back(
        short_query, short_keys, short_values, short_valid, short_high, short_total, short_up
    )
    query_grad = join_heads(long_grads[0], short_grads[0]).astype(jnp.bfloat16)
    key_grad = join_heads(long_grads[1], short_grads[1]).astype(jnp.bfloat16)
    value_grad = join_heads(long_grads[2], short_grads[2]).astype(jnp.bfloat16)
    query_bias_grad = jnp.sum(query_grad.astype(jnp.float32), axis=0)
    value_bias_grad = jnp.sum(value_grad.astype(jnp.float32), axis=0)
    query_weight_grad = jnp.dot(tokens.T, query_grad, preferred_element_type=jnp.float32)
    key_weight_grad = jnp.dot(tokens.T, key_grad, preferred_element_type=jnp.float32)
    value_weight_grad = jnp.dot(tokens.T, value_grad, preferred_element_type=jnp.float32)
    input_part = (
        jnp.dot(query_grad, query_weight.T, preferred_element_type=jnp.float32)
        + jnp.dot(key_grad, key_weight.T, preferred_element_type=jnp.float32)
        + jnp.dot(value_grad, value_weight.T, preferred_element_type=jnp.float32)
    )
    input_grad = (
        lax.psum(input_part.astype(jnp.bfloat16), "tensor").astype(jnp.float32) + resid_one_grad
    )
    (
        query_weight_grad,
        key_weight_grad,
        value_weight_grad,
        inner_weight_grad,
        attn_gain_grad,
        attn_shift_grad,
        output_bias_grad,
        outer_bias_grad,
        ffn_gain_grad,
        ffn_shift_grad,
    ) = (
        lax.psum_scatter(query_weight_grad, "dp", scatter_dimension=0, tiled=True),
        lax.psum_scatter(key_weight_grad, "dp", scatter_dimension=0, tiled=True),
        lax.psum_scatter(value_weight_grad, "dp", scatter_dimension=0, tiled=True),
        lax.psum_scatter(inner_weight_grad, "dp", scatter_dimension=0, tiled=True),
        lax.psum_scatter(attn_gain_grad, "dp", scatter_dimension=0, tiled=True),
        lax.psum_scatter(attn_shift_grad, "dp", scatter_dimension=0, tiled=True),
        lax.psum_scatter(output_bias_grad, "dp", scatter_dimension=0, tiled=True),
        lax.psum_scatter(outer_bias_grad, "dp", scatter_dimension=0, tiled=True),
        lax.psum_scatter(ffn_gain_grad, "dp", scatter_dimension=0, tiled=True),
        lax.psum_scatter(ffn_shift_grad, "dp", scatter_dimension=0, tiled=True),
    )
    output_weight_grad, outer_weight_grad = (
        lax.psum_scatter(output_weight_grad, "dp", scatter_dimension=1, tiled=True),
        lax.psum_scatter(outer_weight_grad, "dp", scatter_dimension=1, tiled=True),
    )
    query_bias_grad, value_bias_grad, inner_bias_grad = lax.psum(
        (query_bias_grad, value_bias_grad, inner_bias_grad), "dp"
    )
    return (
        result,
        pooled,
        input_grad,
        query_weight_grad,
        query_bias_grad,
        key_weight_grad,
        value_weight_grad,
        value_bias_grad,
        output_weight_grad,
        output_bias_grad,
        attn_gain_grad,
        attn_shift_grad,
        inner_weight_grad,
        inner_bias_grad,
        outer_weight_grad,
        outer_bias_grad,
        ffn_gain_grad,
        ffn_shift_grad,
    )


def solution(mesh):
    in_specs = (
        P("dp", None),
        P("dp", None),
        P("dp"),
        P("dp"),
        P("dp", None),
        P(None, "tensor"),
        P("tensor"),
        P(None, "tensor"),
        P(None, "tensor"),
        P("tensor"),
        P("tensor", None),
        P(),
        P(),
        P(),
        P(None, "tensor"),
        P("tensor"),
        P("tensor", None),
        P(),
        P(),
        P(),
    )
    out_specs = (
        P("dp", None),
        P("dp", None),
        P("dp", None),
        P("dp", "tensor"),
        P("tensor"),
        P("dp", "tensor"),
        P("dp", "tensor"),
        P("tensor"),
        P("tensor", "dp"),
        P("dp"),
        P("dp"),
        P("dp"),
        P("dp", "tensor"),
        P("tensor"),
        P("tensor", "dp"),
        P("dp"),
        P("dp"),
        P("dp"),
    )
    return jax.shard_map(
        per_device, mesh=mesh, in_specs=in_specs, out_specs=out_specs, check_vma=False
    )
```

profile of v0, /device:TPU:0, one launch (start us, length us, event | category | flops | bytes accessed | tf_op | source)
XLA Modules:
  0.0 1170.6 jit_solution(7445446376394797641)
XLA Ops:
  13.6 3.9 add_convert_fusion.1
  23.3 3.4 reshape.232
  26.7 3.8 add_convert_fusion.2
  38.6 3.3 reshape.231
  41.9 3.8 convolution_convert_fusion.4
  47.0 2.3 copy.118
  53.8 3.2 reshape.233
  63.8 10.7 fusion.148
  74.5 6.0 fusion.72
  83.0 3.5 convolution_convert_fusion
  86.6 26.0 %all-reduce.12.cloned.1.call-done = bf16[2048,768]{1,0:T(8,128)(2,1)} async-done(((bf16[2048,768]{1,0:T(8,128)(2,1)}), bf16[2048,768]{1,0:T(8,128)(2,1)}) %all-reduce.12.cloned.1.call-update) | async-done | bytes 3145744 | tf_op jit(solution)/shard_map/psum | solution.py:139
  112.6 4.1 fusion.31
  119.5 9.6 multiply_convert_fusion
  129.1 2.7 copy-done.55
  131.8 6.3 convolution_convert_fusion.2
  138.2 24.5 %all-reduce.14.cloned.1.call-done = bf16[2048,768]{1,0:T(8,128)(2,1)} async-done(((bf16[2048,768]{1,0:T(8,128)(2,1)}), bf16[2048,768]{1,0:T(8,128)(2,1)}) %all-reduce.14.cloned.1.call-update) | async-done | bytes 3145744 | tf_op jit(solution)/shard_map/psum | solution.py:155
  162.7 5.2 fusion.141
  169.8 3.6 fusion.20
  173.4 5.0 fusion.140
  178.4 13.8 %convert_reduce_fusion = (f32[1536]{0:T(1024)}, bf16[2048,1536]{1,0:T(8,128)(2,1)S(1)}) fusion(f32[2048,1536]{1,0:T(8,128)} %get-tuple-element.122, f32[1536]{0:T(1024)S(1)} %copy-done.51, bf16[1536,768]{1,0:T(8,128)(2,1)S(1)} %copy-done.50, f32[2048,768]{1,0:T(8,128)S(1)} %get-tuple-element.100), kind=kOutput, calls=%fused_computation.11 | convolution fusion | flops 4874304000 | bytes 27537408 | tf_op jit(solution)/shard_map/dot_general | solution.py:177
  192.2 2.7 copy-done.56
  194.9 6.5 convolution_convert_fusion.1
  201.4 24.5 %all-reduce.16.cloned.1.call-done = bf16[2048,768]{1,0:T(8,128)(2,1)} async-done(((bf16[2048,768]{1,0:T(8,128)(2,1)}), bf16[2048,768]{1,0:T(8,128)(2,1)}) %all-reduce.16.cloned.1.call-update) | async-done | bytes 3145744 | tf_op jit(solution)/shard_map/psum | solution.py:185
  225.9 11.9 %multiply_reduce_fusion.1 = (f32[768]{0:T(1024)}, f32[2048]{0:T(1024)S(1)}, f32[2048]{0:T(1024)S(1)}, f32[768]{0:T(1024)}, f32[768]{0:T(1024)}) fusion(f32[2048,768]{1,0:T(8,128)} %copy-done.5, bf16[2048,768]{1,0:T(8,128)(2,1)} %all-reduce.16.cloned.1.call-done, f32[2048]{0:T(1024)S(1)} %add_rsqrt_fusion.1, f32[2048]{0:T(1024)S(1)} %broadcast_multiply_fusion.5, ...), kind=kLoop, calls=%fused_computation.31 | loop fusion | flops 28305152 | bytes 15776768 | tf_op jit(solution)/shard_map/reduce_sum | solution.py:32
  237.8 7.3 convert_reduce_fusion.3
  248.6 4.1 fusion.82
  255.0 6.6 fusion.83
  261.7 6.9 fusion.86
  269.4 7.6 fusion.69
  277.0 6.3 fusion.99
  283.3 21.0 %fusion.75 = bf16[2,512,6,64]{1,3,2,0:T(8,128)(2,1)S(1)} fusion(f32[2,6,512,512]{2,3,1,0:T(8,128)} %fusion.99, pred[2,512]{1,0:T(4,128)(4,1)S(1)} %get-tuple-element.112, bf16[2,512,6,64]{1,0,3,2:T(2,128)(2,1)S(1)} %copy-done.19, f32[2,6,512,512]{2,3,1,0:T(8,128)} %get-tuple-element.118, f32[2,6,512]{2,1,0:T(8,128)S(1)} %get-tuple-element.117), kind=kOutput, calls=%fused_computation.100 | convolution fusion | flops 425466368 | bytes 26764288 | tf_op jit(solution)/shard_map/bhqk,bkhd->bqhd/dot_general | solution.py:80
  304.4 21.4 %fusion.78 = bf16[2,512,6,64]{1,3,2,0:T(8,128)(2,1)} fusion(f32[2,6,512,512]{2,3,1,0:T(8,128)} %fusion.99, pred[2,512]{1,0:T(4,128)(4,1)S(1)} %get-tuple-element.112, bf16[2,512,6,64]{1,0,3,2:T(2,128)(2,1)S(1)} %copy-done.18, f32[2,6,512,512]{2,3,1,0:T(8,128)} %get-tuple-element.118, f32[2,6,512]{2,1,0:T(8,128)S(1)} %get-tuple-element.117), kind=kOutput, calls=%fused_computation.101 | convolution fusion | flops 425466368 | bytes 26764288 | tf_op jit(solution)/shard_map/bhqk,bqhd->bkhd/dot_general | solution.py:84
  337.1 3.7 add_convert_fusion
  341.0 6.1 fusion.127
  347.2 4.7 convolution_bitcast_fusion
  353.4 3.7 convolution_bitcast_fusion.1
  358.6 3.5 convolution_bitcast_fusion.2
  363.6 10.6 fusion.130
  374.9 12.5 %fusion.89 = f32[768,1536]{1,0:T(8,128)} fusion(bf16[2048,1536]{1,0:T(8,128)(2,1)} %copy-done.56, f32[768]{0:T(1024)S(1)} %copy-done.46, f32[768]{0:T(1024)S(1)} %copy-done.32, bf16[2048,768]{1,0:T(8,128)(2,1)} %all-reduce.12.cloned.1.call-done, bf16[2048,768]{1,0:T(8,128)(2,1)} %param.20, f32[2048]{0:T(1024)S(1)} %add_rsqrt_fusion.1, ...), kind=kOutput, calls=%fused_computation.106 | convolution fusion | flops 4845993984 | bytes 17327104 | tf_op jit(solution)/shard_map/dot_general | solution.py:183
  389.3 3.3 fusion.142
  394.9 77.2 %all-reduce.6 = (f32[384]{0:T(512)}, f32[384]{0:T(512)}, f32[768]{0:T(1024)S(1)}, f32[768]{0:T(1024)S(1)}, f32[768]{0:T(1024)S(1)}, /*index=5*/f32[1536]{0:T(102...) all-reduce(f32[384]{0:T(512)S(1)} %convert_reduce_fusion.5, ...), channel_id=1, replica_groups=mesh['dp'=16,'tensor'=2] {'dp'}, use_global_device_ids=true, to_apply=%region_22.23 | all-reduce | flops 6912 | bytes 55296 | tf_op jit(solution)/shard_map/psum | solution.py:252
  475.6 7.2 convert_add_fusion
  482.7 12.7 %reduce-scatter.13.cloned.1.call-done = f32[384,48]{0,1:T(8,128)} async-done(((f32[384,768]{0,1:T(8,128)}), f32[384,48]{0,1:T(8,128)}) %reduce-scatter.13.cloned.1.call-update) | async-done | bytes 73744 | tf_op jit(solution)/shard_map/reduce_scatter | solution.py:249
  495.4 127.9 %reduce-scatter.23.cloned.1.call-done = f32[48,384]{1,0:T(8,128)} async-done(((f32[768,384]{1,0:T(8,128)}), f32[48,384]{1,0:T(8,128)}) %reduce-scatter.23.cloned.1.call-update) | async-done | bytes 73744
  623.3 127.9 %reduce-scatter.21.cloned.1.call-done = f32[48,384]{1,0:T(8,128)} async-done(((f32[768,384]{1,0:T(8,128)}), f32[48,384]{1,0:T(8,128)}) %reduce-scatter.21.cloned.1.call-update) | async-done | bytes 73744
  751.2 128.0 %reduce-scatter.19.cloned.1.call-done = f32[48,384]{1,0:T(8,128)} async-done(((f32[768,384]{1,0:T(8,128)}), f32[48,384]{1,0:T(8,128)}) %reduce-scatter.19.cloned.1.call-update) | async-done | bytes 73744
  879.2 141.8 %reduce-scatter.17.cloned.1.call-done = f32[1536,48]{0,1:T(8,128)} async-done(((f32[1536,768]{0,1:T(8,128)}), f32[1536,48]{0,1:T(8,128)}) %reduce-scatter.17.cloned.1.call-update) | async-done | bytes 294928 | tf_op jit(solution)/shard_map/reduce_scatter | solution.py:250
  1020.9 142.6 %reduce-scatter.15.cloned.1.call-done = f32[48,1536]{1,0:T(8,128)} async-done(((f32[768,1536]{1,0:T(8,128)}), f32[48,1536]{1,0:T(8,128)}) %reduce-scatter.15.cloned.1.call-update) | async-done | bytes 294928 | tf_op jit(solution)/shard_map/reduce_scatter | solution.py:240
  (207 shorter events, 69.8 us)
Async XLA Ops:
  7.2 112.2 %copy-start = (bf16[768,1536]{1,0:T(8,128)(2,1)S(1)}, bf16[768,1536]{1,0:T(8,128)(2,1)}, u32[]{:S(2)}) copy-start(bf16[768,1536]{1,0:T(8,128)(2,1)} %param.34) | copy-start | bytes 7077892
  7.2 105.4 %all-reduce.12.cloned.1.call-start = ((), (), s32[]{:S(2)}) async-start(), calls=%async_computation.6 | async-start | bytes 6291456 | tf_op jit(solution)/shard_map/psum | solution.py:139
  17.5 9.2 copy-start.52
  80.6 2.4 copy-start.24
  83.0 29.6 %copy-start.29 = (f32[768]{0:T(1024)S(1)}, f32[768]{0:T(1024)}, u32[]{:S(2)}) copy-start(f32[768]{0:T(1024)} %param.31) | copy-start | bytes 9220
  86.5 76.2 %all-reduce.14.cloned.1.call-start = ((), (), s32[]{:S(2)}) async-start(), calls=%async_computation.7 | async-start | bytes 6291456 | tf_op jit(solution)/shard_map/psum | solution.py:155
  112.6 4.1 copy-start.3
  112.6 4.7 copy-start.4
  116.6 2.8 copy-start.31
  116.7 2.8 copy-start.45
  116.7 2.8 copy-start.51
  119.4 12.4 %copy-start.49 = (bf16[1536,768]{1,0:T(8,128)(2,1)S(1)}, bf16[1536,768]{1,0:T(8,128)(2,1)}, u32[]{:S(2)}) copy-start(bf16[1536,768]{1,0:T(8,128)(2,1)} %param.36) | copy-start | bytes 7077892
  129.1 2.7 copy-start.55
  131.8 30.9 %copy-start.43 = (f32[768]{0:T(1024)S(1)}, f32[768]{0:T(1024)}, u32[]{:S(2)}) copy-start(f32[768]{0:T(1024)} %param.37) | copy-start | bytes 9220
  138.2 87.7 %all-reduce.16.cloned.1.call-start = ((), (), s32[]{:S(2)}) async-start(), calls=%async_computation.8 | async-start | bytes 6291456 | tf_op jit(solution)/shard_map/psum | solution.py:185
  169.8 3.6 copy-start.44
  173.4 5.0 copy-start.50
  178.4 13.8 %copy-start.5 = (f32[2048,768]{1,0:T(8,128)}, f32[2048,768]{1,0:T(8,128)S(1)}, u32[]{:S(2)}) copy-start(f32[2048,768]{1,0:T(8,128)S(1)} %get-tuple-element.100) | copy-start | bytes 18874372
  192.2 2.7 copy-start.56
  201.3 274.2 %all-reduce.18.cloned.1.call-start = ((), (), s32[]{:S(2)}) async-start(), calls=%async_computation.9 | async-start | bytes 6291456 | tf_op jit(solution)/shard_map/psum | solution.py:223
  225.9 11.9 %copy-start.7 = (bf16[2048,768]{1,0:T(8,128)(2,1)S(1)}, bf16[2048,768]{1,0:T(8,128)(2,1)}, u32[]{:S(2)}) copy-start(bf16[2048,768]{1,0:T(8,128)(2,1)} %all-reduce.16.cloned.1.call-done) | copy-start | bytes 9437188
  237.8 7.3 copy-start.25
  245.1 3.0 copy-start.2
  248.6 4.1 copy-start.14
  248.6 6.4 copy-start.15
  261.7 6.9 copy-start.17
  269.4 7.6 copy-start.12
  277.0 6.3 copy-start.19
  283.3 21.0 %copy-start.18 = (bf16[2,512,6,64]{1,0,3,2:T(2,128)(2,1)S(1)}, bf16[2,512,6,64]{1,0,3,2:T(2,128)(2,1)}, u32[]{:S(2)}) copy-start(bf16[2,512,6,64]{1,0,3,2:T(2,128)(2,1)} %reshape.232) | copy-start | bytes 2359300
  304.4 21.4 %copy-start.22 = (bf16[8,128,6,64]{1,3,2,0:T(8,128)(2,1)S(1)}, bf16[8,128,6,64]{1,3,2,0:T(8,128)(2,1)}, u32[]{:S(2)}) copy-start(bf16[8,128,6,64]{1,3,2,0:T(8,128)(2,1)} %fusion.82) | copy-start | bytes 2359300
  325.8 2.9 copy-start.21
  325.8 3.4 copy-start.20
  325.8 3.9 copy-start.23
  333.9 3.2 copy-start.28
  340.8 154.6 %reduce-scatter.13.cloned.1.call-start = ((), (), s32[]{:S(2)}) async-start(), calls=%async_computation.10 | async-start | bytes 1253376 | tf_op jit(solution)/shard_map/reduce_scatter | solution.py:249
  347.2 276.1 %reduce-scatter.23.cloned.1.call-start = ((), (), s32[]{:S(2)}) async-start(), calls=%async_computation.15 | async-start | bytes 1253376
  353.3 397.8 %reduce-scatter.21.cloned.1.call-start = ((), (), s32[]{:S(2)}) async-start(), calls=%async_computation.14 | async-start | bytes 1253376
  358.6 520.6 %reduce-scatter.19.cloned.1.call-start = ((), (), s32[]{:S(2)}) async-start(), calls=%async_computation.13 | async-start | bytes 1253376
  363.5 657.4 %reduce-scatter.17.cloned.1.call-start = ((), (), s32[]{:S(2)}) async-start(), calls=%async_computation.12 | async-start | bytes 5013504 | tf_op jit(solution)/shard_map/reduce_scatter | solution.py:250
  374.2 789.4 %reduce-scatter.15.cloned.1.call-start = ((), (), s32[]{:S(2)}) async-start(), calls=%async_computation.11 | async-start | bytes 5013504 | tf_op jit(solution)/shard_map/reduce_scatter | solution.py:240
  389.3 3.4 copy-start.40
  389.3 3.7 copy-start.48
  389.3 3.8 copy-start.39
  392.7 2.1 copy-start.34
  392.7 2.1 copy-start.35
  392.7 2.1 copy-start.36
  392.7 2.1 copy-start.37
  475.0 688.6 %copy-start.1 = (bf16[768,1536]{1,0:T(8,128)(2,1)S(1)}, bf16[768,1536]{1,0:T(8,128)(2,1)}, u32[]{:S(2)}) copy-start(bf16[768,1536]{1,0:T(8,128)(2,1)} %param.34) | copy-start | bytes 7077892
  (19 other events, 27.6 us)
Sparse Core Ops, SparseCore 0:
  86.6 25.8 all-reduce.11
  138.3 24.3 all-reduce.13
  201.5 24.3 all-reduce.15
  340.9 24.3 all-reduce.17
  370.5 124.8 reduce-scatter.12
  500.6 122.6 reduce-scatter.22
  628.6 122.5 reduce-scatter.20
  756.5 122.6 reduce-scatter.18
  884.9 135.9 reduce-scatter.16
  1027.4 136.1 reduce-scatter.14
where the time goes:
time: 1170 us
  waiting for transfers between devices  756 us (65%)
  matrix products  197 us (17%)
  blocking collectives  77.2 us (7%)
  local copies, waits for them, and re-layouts  67.8 us (6%)
  other arithmetic  56.2 us (5%)
  between operations  15.9 us (1%)
    unnamed x13, waiting for transfers between devices  384 us
    reduce_scatter x1, waiting for transfers between devices, per_device(): lax.psum_scatter(inner_weight_grad, 'dp', scatter_dimension=0, tiled=True)  143 us
    reduce_scatter x1, waiting for transfers between devices, per_device(): lax.psum_scatter(outer_weight_grad, 'dp', scatter_dimension=1, tiled=True)  142 us
    psum x1, blocking collectives, per_device(): lax.psum((query_bias_grad, value_bias_grad, inner_bias_grad), 'dp')  77.2 us
    dot_general x2, matrix products, attend_back(): jnp.einsum('bhqk,bqhd->bkhd', score_grad, queries, preferred_element_type...  28.3 us
    dot_general x2, matrix products, attend_back(): jnp.einsum('bhqk,bkhd->bqhd', score_grad, keys_in, preferred_element_type...  27.7 us
    unnamed x136, local copies, waits for them, and re-layouts  26.6 us
    psum x1, waiting for transfers between devices, per_device(): lax.psum(jnp.dot(heads_low, output_weight, preferred_element_type=jnp.flo...  26 us
  transfers between devices with their start and end apart: 10, of which 9 were waited for; matrix products, arithmetic and copies ran while one was open for 5% of the time, Pallas kernels for 0%

commit v1 on v0

v1 whole, which is shorter than its diff:
```python
import functools

import jax
import jax.numpy as jnp
from jax import lax
from jax.experimental import pallas as pl
from jax.experimental.pallas import tpu as pltpu
from jax.sharding import PartitionSpec as P

HEAD_DIM = 64
LONG = 512
SHORT = 128
PAIR = 128
NORM_EPS = 1e-12
MASKED = -1000000000.0
SCORE_SCALE = 0.125
INV_ROOT_TAU = 0.3989422804014327
ROOT_HALF = 0.7071067811865476
BF = jnp.bfloat16
F32 = jnp.float32
MESH = pl.DeviceIdType.MESH
UNIT = 384
BITS = 4
GROUPS = 1 << BITS

VM = pl.BlockSpec(memory_space=pltpu.VMEM)
SM = pl.BlockSpec(memory_space=pltpu.SMEM)
ANY = pl.BlockSpec(memory_space=pl.ANY)


def params(**more):
    return pltpu.CompilerParams(vmem_limit_bytes=58 << 20, **more)


def dot(a, b):
    return jnp.dot(a, b, preferred_element_type=F32)


def dot_nt(a, b):
    return lax.dot_general(a, b, (((1,), (1,)), ((), ())), preferred_element_type=F32)


def dot_tn(a, b):
    return lax.dot_general(a, b, (((0,), (0,)), ((), ())), preferred_element_type=F32)


def spans(start, unit, size=None):
    return pl.ds(pl.multiple_of(start, unit), unit if size is None else size)


def my_slots(long_ref, short_ref, count_ref):
    tensor = lax.axis_index("tensor")
    n_long, n_short = long_ref.shape[0] // 2, short_ref.shape[0] // 2
    lengths = []
    for ref, n, column in ((long_ref, n_long, 0), (short_ref, n_short, 1)):
        for j in range(n):
            slot = tensor * n + j
            lengths.append(jnp.where(slot < count_ref[0, column], ref[slot], 0))
    return lengths


def my_rows(whole_ref, mine_ref, sem):
    tensor = lax.axis_index("tensor")
    half = mine_ref.shape[0] // 2
    return [
        pltpu.make_async_copy(
            whole_ref.at[pl.ds(pl.multiple_of((2 * k + tensor) * half, half), half)],
            mine_ref.at[pl.ds(k * half, half)], sem.at[k])
        for k in range(2)
    ]


def key_terms(length, count):
    keys = lax.broadcasted_iota(jnp.int32, (1, count), 1)
    scale = jnp.where(length > 0, SCORE_SCALE, 0.0).astype(BF)
    bias = jnp.where((keys < length) | (length <= 0), 0.0, MASKED)
    return scale, bias


def halves():
    return lax.broadcasted_iota(jnp.int32, (1, PAIR), 1) // HEAD_DIM


def attend_kernel(
    long_ref, short_ref, count_ref, tok_ref, wq_ref, wk_ref, wv_ref, bias_ref, qkv_ref, a_ref, lse_ref, wc_ref,
    x_ref, sem,
):
    loads = my_rows(tok_ref, x_ref, sem)
    for load in loads:
        load.start()
    lengths = my_slots(long_ref, short_ref, count_ref)
    rows_all, width = qkv_ref.shape
    pairs = width // (3 * PAIR)
    inner = pairs * PAIR
    for p in range(pairs):
        cols = slice(p * PAIR, (p + 1) * PAIR)
        for k, w_ref in enumerate((wq_ref, wk_ref, wv_ref)):
            wc_ref[:, (3 * p + k) * PAIR:(3 * p + k + 1) * PAIR] = w_ref[:, cols]
    for load in loads:
        load.wait()
    for p in range(pairs):
        cols = slice(p * 384, (p + 1) * 384)
        value = dot(x_ref[...], wc_ref[:, cols])
        bq = bias_ref[0:1, p * PAIR:(p + 1) * PAIR]
        bv = bias_ref[0:1, inner + p * PAIR:inner + (p + 1) * PAIR]
        qkv_ref[:, cols] = (value + jnp.concatenate([bq, jnp.zeros_like(bq), bv], axis=1)).astype(BF)
    half = halves()
    lane = lax.broadcasted_iota(jnp.int32, (1, PAIR), 1)
    lse_ref[...] = jnp.zeros_like(lse_ref)

    def block(row0, count, length, p):
        rows = slice(row0, row0 + count)
        scale, bias = key_terms(length, count)
        qp = qkv_ref[rows, spans(p * 384, 128)] * scale
        kp = qkv_ref[rows, spans(p * 384 + 128, 128)]
        vp = qkv_ref[rows, spans(p * 384 + 256, 128)]
        out = None
        stat = lse_ref[rows, :]
        for h in range(2):
            own = half == h
            s = dot_nt(jnp.where(own, qp, jnp.zeros_like(qp)), kp) + bias
            high = jnp.max(s, axis=1, keepdims=True)
            e = jnp.exp(s - high)
            total = jnp.sum(e, axis=1, keepdims=True)
            o = dot(e.astype(BF), jnp.where(own, vp, jnp.zeros_like(vp))) * (1.0 / total)
            out = o if out is None else out + o
            stat = jnp.where(lane == p * 2 + h, high + jnp.log(total), stat)
        a_ref[rows, spans(p * 128, 128)] = out.astype(BF)
        lse_ref[rows, :] = stat

    def pair(p, _):
        block(0, LONG, lengths[0], p)
        for s in range((rows_all - LONG) // SHORT):
            block(LONG + SHORT * s, SHORT, lengths[1 + s], p)
        return 0

    lax.fori_loop(0, pairs, pair, 0)


def attend(slots, tokens, weights, bias):
    rows, d = tokens.shape[0] // 2, tokens.shape[1]
    inner = weights[0].shape[1]
    shape = jax.ShapeDtypeStruct
    return pl.pallas_call(
        attend_kernel,
        out_shape=(
            shape((rows, 3 * inner), BF), shape((rows, inner), BF), shape((rows, 128), F32), shape((d, 3 * inner), BF),
        ),
        in_specs=[SM, SM, SM, ANY, VM, VM, VM, VM],
        out_specs=(VM,) * 4,
        scratch_shapes=[pltpu.VMEM((rows, d), BF), pltpu.SemaphoreType.DMA((2,))],
        compiler_params=params(),
        cost_estimate=pl.CostEstimate(
            flops=6 * rows * d * inner + 8 * rows * 512 * inner, bytes_accessed=8 << 20, transcendentals=rows * 512 * 6),
        name="attend",
    )(*slots, tokens, *weights, bias)


def norm(v, gain, shift):
    centre = v - jnp.mean(v, axis=-1, keepdims=True)
    inverse = lax.rsqrt(jnp.mean(centre * centre, axis=-1, keepdims=True) + NORM_EPS)
    normed = centre * inverse
    return normed * gain + shift, normed, inverse


def norm_back(e, normed, inverse, gain):
    scaled = e * gain
    plain = jnp.mean(scaled, axis=-1, keepdims=True)
    cross = jnp.mean(scaled * normed, axis=-1, keepdims=True)
    return inverse * (scaled - plain - normed * cross)


def gelu_terms(u):
    t = 1.0 / (1.0 + (0.3275911 * ROOT_HALF) * jnp.abs(u))
    bell = jnp.exp(-0.5 * u * u)
    poly = t * (0.127414796 + t * (-0.142248368 + t * (0.7107068705 + t * (-0.7265760135 + t * 0.5307027145))))
    tail = poly * bell
    cdf = jnp.where(u >= 0.0, 1.0 - tail, tail)
    return u * cdf, cdf + u * bell * INV_ROOT_TAU


def forward_kernel(
    long_ref, short_ref, count_ref, x_ref, cot_ref, ao_ref, ap_ref, woo_ref, wop_ref,
    w1o_hbm, w1p_hbm, w2o_hbm, w2p_hbm, bo_ref, bp_ref,
    attn_bias_ref, a1_ref, s1_ref, ffn_bias_ref, a2_ref, s2_ref,
    result_ref, pooled_ref, n1_ref, r1_ref, h_ref, go_ref, gp_ref, do_ref, dp_ref, df_ref, dr_ref, grad_ref,
    w1o_ref, w1p_ref, w2o_ref, w2p_ref, sem,
):
    step = pl.program_id(0)
    loads = [
        pltpu.make_async_copy(src, dst, sem.at[k]) for k, (src, dst) in enumerate(
            ((w1o_hbm, w1o_ref), (w1p_hbm, w1p_ref), (w2o_hbm, w2o_ref), (w2p_hbm, w2p_ref)))]

    @pl.when(step == 0)
    def _():
        for load in loads:
            load.start()

    lengths = my_slots(long_ref, short_ref, count_ref)
    rows_all = x_ref.shape[0]
    skip = bo_ref.shape[1] - w1o_ref.shape[1]
    width = w1o_ref.shape[1]
    tile = 256
    chunk = 512
    attn_bias, a1, s1, ffn_bias, a2, s2 = (
        ref[...] for ref in (attn_bias_ref, a1_ref, s1_ref, ffn_bias_ref, a2_ref, s2_ref))

    @pl.when(step == 0)
    def _():
        grad_ref[...] = jnp.zeros_like(grad_ref)

    pooled_ref[...] = jnp.zeros_like(pooled_ref)

    def head(i, _):
        rows = spans(i * tile, tile)
        attn = dot(ao_ref[rows, :], woo_ref[...]) + dot(ap_ref[rows, :], wop_ref[...]) + attn_bias
        h1, normed, inverse = norm(x_ref[rows, :].astype(F32) + attn, a1, s1)
        n1_ref[rows, :] = normed
        r1_ref[rows, :] = jnp.broadcast_to(inverse, (tile, 128))
        h_ref[rows, :] = h1.astype(BF)
        return 0

    lax.fori_loop(0, rows_all // tile, head, 0)

    for k, (w1_ref, b1_ref, g_ref, d_ref) in enumerate(
            ((w1o_ref, bo_ref, go_ref, do_ref), (w1p_ref, bp_ref, gp_ref, dp_ref))):
        pl.when(step == 0)(loads[k].wait)

        def inner(c, _, w1_ref=w1_ref, b1_ref=b1_ref, g_ref=g_ref, d_ref=d_ref):
            cols = spans(c * chunk, chunk)
            for i in range(rows_all // tile):
                rows = slice(i * tile, (i + 1) * tile)
                u = dot(h_ref[rows, :], w1_ref[:, cols]) + b1_ref[:, spans(skip + c * chunk, 128, chunk)]
                g, slope = gelu_terms(u)
                g_ref[rows, cols] = g.astype(BF)
                d_ref[rows, cols] = slope.astype(BF)
            return 0

        lax.fori_loop(0, width // chunk, inner, 0)

    @pl.when(step == 0)
    def _():
        loads[2].wait()
        loads[3].wait()

    def tail(i, _):
        rows = spans(i * tile, tile)
        ffn = dot(go_ref[rows, :], w2o_ref[...]) + dot(gp_ref[rows, :], w2p_ref[...]) + ffn_bias
        h1 = n1_ref[rows, :] * a1 + s1
        y, normed, inverse = norm(h1 + ffn, a2, s2)
        result_ref[rows, :] = y.astype(BF)
        place = i * tile + lax.broadcasted_iota(jnp.int32, (tile, 1), 0)

        @pl.when(step == 0)
        def _():
            pooled_ref[0:1, :] += jnp.sum(jnp.where(place < lengths[0], y, 0.0), axis=0, keepdims=True)

        @pl.when(step == 1)
        def _():
            local = lax.broadcasted_iota(jnp.int32, (SHORT, 1), 0)
            per = tile // SHORT
            for k in range(per):
                slot = i * per + k
                length = jnp.where(i == 0, lengths[1 + k], lengths[1 + per + k])
                part = jnp.where(local < length, y[k * SHORT:(k + 1) * SHORT, :], 0.0)
                pooled_ref[pl.ds(slot, 1), :] = jnp.sum(part, axis=0, keepdims=True)

        e = cot_ref[rows, :].astype(F32)
        dr = norm_back(e, normed, inverse, a2)
        low = dr.astype(BF)
        dr_ref[rows, :] = dr
        df_ref[rows, :] = low
        grad_ref[0:1, :] += jnp.sum(low.astype(F32), axis=0, keepdims=True)
        grad_ref[1:2, :] += jnp.sum(e * normed, axis=0, keepdims=True)
        grad_ref[2:3, :] += jnp.sum(e, axis=0, keepdims=True)
        return 0

    lax.fori_loop(0, rows_all // tile, tail, 0)

    @pl.when(step == 0)
    def _():
        pooled_ref[0:1, :] = pooled_ref[0:1, :] / jnp.maximum(lengths[0], 1).astype(F32)

    @pl.when(step == 1)
    def _():
        for s in range(4):
            pooled_ref[s:s + 1, :] = pooled_ref[s:s + 1, :] / jnp.maximum(lengths[1 + s], 1).astype(F32)


def forward(slots, tokens, cot, ao, ap, wo, w1, w2, b1, vectors):
    rows, d = tokens.shape[0] // 2, tokens.shape[1]
    width = w1[0].shape[1]
    blk = rows // 2

    def row(cols):
        return pl.BlockSpec((blk, cols), lambda i: (i, 0))

    def picked(cols):
        return pl.BlockSpec((blk, cols), lambda i: (2 * i + lax.axis_index("tensor"), 0))

    def whole(a):
        return pl.BlockSpec(a.shape, lambda i: (0, 0), pipeline_mode=pl.Buffered(1))

    shape = jax.ShapeDtypeStruct
    return pl.pallas_call(
        forward_kernel,
        grid=(2,),
        out_shape=(
            shape((rows, d), BF), shape((16, d), F32), shape((rows, d), F32), shape((rows, 128), F32),
            shape((rows, d), BF), shape((rows, width), BF), shape((rows, width), BF), shape((rows, width), BF),
            shape((rows, width), BF), shape((rows, d), BF), shape((rows, d), F32), shape((8, d), F32),
        ),
        in_specs=[SM, SM, SM, picked(d), picked(d), row(ao.shape[1]), row(ao.shape[1])]
        + [whole(a) for a in wo] + [ANY] * 4 + [whole(a) for a in (*b1, *vectors)],
        out_specs=(
            row(d), pl.BlockSpec((8, d), lambda i: (i, 0)), row(d), row(128), row(d), row(width), row(width),
            row(width), row(width), row(d), row(d), pl.BlockSpec((8, d), lambda i: (0, 0)),
        ),
        scratch_shapes=[
            pltpu.VMEM((d, width), BF), pltpu.VMEM((d, width), BF), pltpu.VMEM((width, d), BF),
            pltpu.VMEM((width, d), BF), pltpu.SemaphoreType.DMA((4,))],
        compiler_params=params(),
        cost_estimate=pl.CostEstimate(flops=2 * rows * d * (width * 4 + d), bytes_accessed=50 << 20, transcendentals=rows * width * 4),
        name="forward",
    )(*slots, tokens, cot, ao, ap, *wo, *w1, *w2, *b1, *vectors)


def peer(sub, bit):
    me = lax.axis_index("dp")
    group = me // sub
    value = (group // (1 << bit)) % 2
    other = me + (1 - 2 * value) * (sub << bit)
    return value, {"dp": other}


def remote(src, dst, s, r, device):
    return pltpu.make_async_remote_copy(
        src_ref=src, dst_ref=dst, send_sem=s, recv_sem=r, device_id=device, device_id_type=MESH)


class Halving:
    orders = ((0, 1, 2, 3), (1, 0, 2, 3))

    def __init__(self, sub, sums, sends, ins, first, s_sem, r_sem):
        self.links = [peer(sub, bit) for bit in range(BITS)]
        self.partner = {"tensor": 1 - lax.axis_index("tensor")}
        self.sums, self.sends, self.ins, self.first = sums, sends, ins, first
        self.s_sem, self.r_sem = s_sem, r_sem
        self.stage = {}
        self.copy = {}

    def greet(self):
        barrier = pltpu.get_barrier_semaphore()
        for device in [self.partner] + [link[1] for link in self.links]:
            pl.semaphore_signal(barrier, inc=1, device_id=device, device_id_type=MESH)

    def meet(self):
        pl.semaphore_wait(pltpu.get_barrier_semaphore(), BITS + 1)

    def region(self, u, count, bit=None):
        fixed = self.orders[u % 2][:count]
        index = [u]
        for b in reversed(range(BITS)):
            value = self.links[b][0]
            index.append(value if b in fixed else 1 - value if b == bit else slice(None))
        return tuple(index)

    def swap(self, u):
        k = u - self.first[0]
        self.stage[u] = 0
        self.copy[u] = remote(
            self.sends.at[k], self.ins[0].at[k], self.s_sem.at[u, BITS], self.r_sem.at[u, BITS], self.partner)
        self.copy[u].start()

    def resume(self, u, stage):
        self.stage[u] = stage

    def arrive(self, u):
        stage = self.stage[u]
        self.copy[u].wait()
        index = self.region(u, stage)
        brought = self.ins[stage][u - self.first[stage]].astype(F32)
        total = self.sums[index].astype(F32) + brought
        if stage == BITS:
            return total
        self.sums[index] = total.astype(BF)
        return None

    def depart(self, u):
        stage = self.stage[u]
        bit = self.orders[u % 2][stage]
        index = self.region(u, stage, bit)
        self.copy[u] = remote(
            self.sums.at[index], self.ins[stage + 1].at[u - self.first[stage + 1]],
            self.s_sem.at[u, stage], self.r_sem.at[u, stage], self.links[bit][1])
        self.copy[u].start()
        self.stage[u] = stage + 1

    def move(self, *units):
        for u in units:
            self.arrive(u)
            self.depart(u)


def halving_scratch(first, units):
    shapes = ((2, 2, 2, 2), (2, 2, 2), (2, 2), (2,), ())
    return [pltpu.VMEM((max(units - f, 1), *s, 48, UNIT), BF) for f, s in zip(first, shapes)] + [
        pltpu.SemaphoreType.DMA((units, BITS + 1)), pltpu.SemaphoreType.DMA((units, BITS + 1))]


def weight_grad(out_ref, units, left_ref, right_ref, cols):
    def part(i, _):
        value = dot_tn(left_ref[:, spans(i * UNIT, UNIT)], right_ref[:, cols]).astype(BF)
        for k, u in enumerate(units):
            out_ref[u, i] = value[:, k * UNIT:(k + 1) * UNIT].reshape(2, 2, 2, 48, UNIT)
        return 0

    lax.fori_loop(0, left_ref.shape[1] // UNIT, part, 0)


FIRST_A = (0, 0, 0, 0, 0)
STAGES_A = (3, 3, 2, 2, 1, 1, 0, 0)


def ffn_back_kernel(
    sub, df_hbm, h_hbm, dr_hbm, gp_hbm, go_hbm, dp_hbm, do_hbm, w1p_hbm, w1o_hbm, w2p_hbm, w2o_hbm,
    sums_out, dh_ref, bp_ref, bo_ref,
    df_ref, h_ref, g_ref, slope_ref, w1_ref, w2_ref, u_ref, sums_ref, send_ref,
    in0_ref, in1_ref, in2_ref, in3_ref, in4_ref, s_sem, r_sem, load_sem, out_sem,
):
    rows_all, d = df_ref.shape
    width = w1_ref.shape[2]
    chunk = 2 * UNIT
    chunks = width // chunk
    tile = 256
    red = Halving(sub, sums_ref, send_ref, (in0_ref, in1_ref, in2_ref, in3_ref, in4_ref), FIRST_A, s_sem, r_sem)
    red.greet()
    loads = {}

    def load(name, src, dst):
        loads[name] = pltpu.make_async_copy(src, dst, load_sem.at[len(loads)])
        loads[name].start()

    def need(*names):
        for name in names:
            loads.pop(name).wait()
            loads[name + "!"] = None

    load("df", df_hbm, df_ref)
    for c in range(chunks):
        cols = pl.ds(c * chunk, chunk)
        for k, hbm in enumerate((gp_hbm, go_hbm)):
            load(f"g{k}{c}", hbm.at[:, cols], g_ref.at[k, :, cols])
    load("h", h_hbm, h_ref)
    for c in range(chunks):
        cols = pl.ds(c * chunk, chunk)
        for k, (w2_hbm, d_hbm) in enumerate(((w2p_hbm, dp_hbm), (w2o_hbm, do_hbm))):
            load(f"w{k}{c}", w2_hbm.at[cols], w2_ref.at[k, cols])
            load(f"d{k}{c}", d_hbm.at[:, cols], slope_ref.at[k, :, cols])
    load("dr", dr_hbm, dh_ref)
    for k, w1_hbm in enumerate((w1p_hbm, w1o_hbm)):
        load(f"i{k}", w1_hbm, w1_ref.at[k])

    bp_ref[...] = jnp.zeros_like(bp_ref)
    bo_ref[...] = jnp.zeros_like(bo_ref)
    need("df")
    for c in range(chunks):
        cols = slice(c * chunk, (c + 1) * chunk)
        units = (2 * c, 2 * c + 1)
        for k, out_ref in enumerate((send_ref, sums_ref)):
            need(f"g{k}{c}")
            weight_grad(out_ref, units, df_ref, g_ref.at[k], cols)
            if k == 0:
                if c == 0:
                    red.meet()
                for u in units:
                    red.swap(u)
        if c == 1:
            red.move(0, 1)
    need("h")
    for c in range(chunks):
        cols = slice(c * chunk, (c + 1) * chunk)
        units = (2 * chunks + 2 * c, 2 * chunks + 2 * c + 1)
        for k, (out_ref, bias_ref) in enumerate(((send_ref, bp_ref), (sums_ref, bo_ref))):
            need(f"w{k}{c}", f"d{k}{c}")

            def part(i, _, k=k, bias_ref=bias_ref, cols=cols):
                rows = spans(i * tile, tile)
                du = (dot_nt(df_ref[rows, :], w2_ref[k, cols, :]) * slope_ref[k, rows, cols].astype(F32)).astype(BF)
                u_ref[k, rows, cols] = du
                bias_ref[0:1, cols] += jnp.sum(du.astype(F32), axis=0, keepdims=True)
                return 0

            lax.fori_loop(0, rows_all // tile, part, 0)
            weight_grad(out_ref, units, h_ref, u_ref.at[k], cols)
            if k == 0:
                for u in units:
                    red.swap(u)
            if (c, k) == (0, 0):
                red.move(2, 3)
            if (c, k) == (1, 0):
                red.move(0, 1)
    need("dr", "i0", "i1")

    def back(i, _):
        rows = spans(i * tile, tile)
        dh_ref[rows, :] += dot_nt(u_ref[0, rows, :], w1_ref[0]) + dot_nt(u_ref[1, rows, :], w1_ref[1])
        return 0

    red.move(4, 5)
    lax.fori_loop(0, rows_all // tile // 2, back, 0)
    red.move(2, 3)
    red.move(0, 1)
    lax.fori_loop(rows_all // tile // 2, rows_all // tile, back, 0)
    for u in range(4 * chunks):
        red.arrive(u)
    outs = pltpu.make_async_copy(sums_ref, sums_out, out_sem)
    outs.start()
    outs.wait()


def ffn_back(sub, df, h, dr, g, slope, w1, w2):
    rows, d = df.shape
    width = w1[0].shape[1]
    units = 2 * width // UNIT
    shape = jax.ShapeDtypeStruct
    return pl.pallas_call(
        functools.partial(ffn_back_kernel, sub),
        out_shape=(
            shape((units, 2, 2, 2, 2, 48, UNIT), BF), shape((rows, d), F32), shape((8, width), F32), shape((8, width), F32),
        ),
        in_specs=[ANY] * 11,
        out_specs=(ANY, VM, VM, VM),
        scratch_shapes=[
            pltpu.VMEM((rows, d), BF), pltpu.VMEM((rows, d), BF), pltpu.VMEM((2, rows, width), BF),
            pltpu.VMEM((2, rows, width), BF), pltpu.VMEM((2, d, width), BF), pltpu.VMEM((2, width, d), BF),
            pltpu.VMEM((2, rows, width), BF),
            pltpu.VMEM((units, 2, 2, 2, 2, 48, UNIT), BF), pltpu.VMEM((units, 2, 2, 2, 2, 48, UNIT), BF),
            *halving_scratch(FIRST_A, units), pltpu.SemaphoreType.DMA((20,)), pltpu.SemaphoreType.DMA,
        ],
        compiler_params=params(collective_id=1, has_side_effects=True),
        name="ffn_back",
    )(df, h, dr, *g, *slope, *w1, *w2)


FIRST_B = (8, 6, 4, 2, 0)


def attn_back_kernel(
    sub, long_ref, short_ref, count_ref, sums_hbm, dh_hbm, n1_hbm, r1_hbm, gain_ref, tok_hbm, qkvp_hbm, qkvo_hbm,
    ap_hbm, ao_hbm, lsep_hbm, lseo_hbm, wop_hbm, woo_hbm, wcp_hbm, wco_hbm, grad2_ref, b1p_ref, b1o_ref,
    outer_ref, inner_ref, q_ref, k_ref, v_ref, output_ref, dx_out, vec_out,
    dx_ref, n1_ref, r1_ref, x_ref, qkv_ref, a_ref, lse_ref, wo_ref, wc_ref, low_ref, da_ref, dqkv_ref,
    grad_ref, vsend_ref, vec_ref, vin_ref, sums_ref, send_ref,
    in0_ref, in1_ref, in2_ref, in3_ref, in4_ref, s_sem, r_sem, vs_sem, vr_sem, load_sem, out_sem, swap_sem,
):
    rows_all, d = dx_ref.shape
    pairs = a_ref.shape[2] // PAIR
    tile = 256
    half = halves()
    lane = lax.broadcasted_iota(jnp.int32, (1, PAIR), 1)
    lengths = my_slots(long_ref, short_ref, count_ref)
    tensor = lax.axis_index("tensor")
    red = Halving(sub, sums_ref, send_ref, (in0_ref, in1_ref, in2_ref, in3_ref, in4_ref), FIRST_B, s_sem, r_sem)
    red.greet()
    loads = []

    def load(src, dst):
        loads.append(pltpu.make_async_copy(src, dst, load_sem.at[len(loads)]))
        loads[-1].start()
        return loads[-1]

    handed = len(STAGES_A)
    pieces = []
    for u, stage in enumerate(STAGES_A):
        red.resume(u, stage)
        index = red.region(u, stage)
        pieces.append(load(sums_hbm.at[index], sums_ref.at[index]))
    norms = [load(dh_hbm, dx_ref), load(n1_hbm, n1_ref), load(r1_hbm, r1_ref)]
    heads = [load(ap_hbm, a_ref.at[0]), load(ao_hbm, a_ref.at[1]), load(wop_hbm, wo_ref.at[0]), load(woo_hbm, wo_ref.at[1])]
    heads += [load(qkvp_hbm, qkv_ref.at[0]), load(qkvo_hbm, qkv_ref.at[1]), load(lsep_hbm, lse_ref.at[0]), load(lseo_hbm, lse_ref.at[1])]
    rows_in = my_rows(tok_hbm, x_ref, load_sem.at[pl.ds(len(loads), 2)])
    for copy in rows_in:
        copy.start()
    loads += rows_in
    last = [load(wcp_hbm, wc_ref.at[0]), load(wco_hbm, wc_ref.at[1])]

    for piece in pieces:
        piece.wait()
    red.meet()
    for u in range(handed):
        red.depart(u)
    final = {}

    def finish(*units):
        for u in units:
            value = red.arrive(u)
            if u < 4:
                outer_ref[u * UNIT:(u + 1) * UNIT, :] = value.T
            elif u < 8:
                inner_ref[:, (u - 4) * UNIT:(u - 3) * UNIT] = value
            elif u == 8:
                output_ref[...] = value.T
            else:
                for i, ref in enumerate((q_ref, k_ref, v_ref)):
                    ref[:, (u - 9) * PAIR:(u - 8) * PAIR] = value[:, i * PAIR:(i + 1) * PAIR]

    for copy in norms:
        copy.wait()
    grad_ref[...] = jnp.zeros_like(grad_ref)

    def first(i, _):
        rows = spans(i * tile, tile)
        e, normed = dx_ref[rows, :], n1_ref[rows, :]
        dr = norm_back(e, normed, r1_ref[rows, 0:1], gain_ref[...])
        low = dr.astype(BF)
        dx_ref[rows, :] = dr
        low_ref[rows, :] = low
        grad_ref[0:1, :] += jnp.sum(low.astype(F32), axis=0, keepdims=True)
        grad_ref[1:2, :] += jnp.sum(e * normed, axis=0, keepdims=True)
        grad_ref[2:3, :] += jnp.sum(e, axis=0, keepdims=True)
        return 0

    lax.fori_loop(0, rows_all // tile, first, 0)
    for copy in heads + rows_in:
        copy.wait()
    weight_grad(send_ref, (0,), low_ref, a_ref.at[0], slice(0, UNIT))
    red.swap(8)
    weight_grad(sums_ref, (8,), low_ref, a_ref.at[1], slice(0, UNIT))

    def lift(i, _):
        rows = spans(i * tile, tile)
        for k in range(2):
            da_ref[k, rows, :] = dot_nt(low_ref[rows, :], wo_ref[k]).astype(BF)
        return 0

    lax.fori_loop(0, rows_all // tile, lift, 0)
    red.move(4, 5)
    red.move(2, 3)
    finish(0, 1)
    red.move(6, 7)

    def block(row0, count, length, k, p):
        rows = slice(row0, row0 + count)
        scale, bias = key_terms(length, count)
        qp = qkv_ref[k, rows, p * 384:p * 384 + 128] * scale
        kp = qkv_ref[k, rows, p * 384 + 128:p * 384 + 256]
        vp = qkv_ref[k, rows, p * 384 + 256:p * 384 + 384]
        dap = da_ref[k, rows, p * 128:p * 128 + 128]
        prod = dap.astype(F32) * a_ref[k, rows, p * 128:p * 128 + 128].astype(F32)
        ks = kp * scale
        stat = lse_ref[k, rows, :]
        dq = dk = dv = None
        for h in range(2):
            own = half == h
            zero = jnp.zeros_like(qp)
            qh, dah = jnp.where(own, qp, zero), jnp.where(own, dap, zero)
            delta = jnp.sum(jnp.where(own, prod, 0.0), axis=1, keepdims=True)
            lse = jnp.sum(jnp.where(lane == p * 2 + h, stat, 0.0), axis=1, keepdims=True)
            prob = jnp.exp(dot_nt(qh, kp) + bias - lse)
            ds = (prob * (dot_nt(dah, vp) - delta)).astype(BF)
            dvh = dot_tn(prob.astype(BF), dah)
            dkh = dot_tn(ds, qh)
            dqh = dot(ds, jnp.where(own, ks, zero))
            dq = dqh if dq is None else dq + dqh
            dk = dkh if dk is None else dk + dkh
            dv = dvh if dv is None else dv + dvh
        dqkv_ref[k, rows, p * 384:p * 384 + 128] = dq.astype(BF)
        dqkv_ref[k, rows, p * 384 + 128:p * 384 + 256] = dk.astype(BF)
        dqkv_ref[k, rows, p * 384 + 256:p * 384 + 384] = dv.astype(BF)

    after = {
        (0, 0): lambda: red.move(8, 4, 5),
        (0, 1): lambda: finish(2, 3),
        (1, 0): lambda: red.move(6, 7, 8, 9),
        (1, 1): lambda: finish(4, 5),
        (2, 0): lambda: red.move(6, 7, 8, 9, 10),
        (2, 1): lambda: None,
    }
    for p in range(pairs):
        for k, out_ref in enumerate((send_ref, sums_ref)):
            def half_pair(k, p=p):
                block(0, LONG, lengths[0], k, p)
                for s in range((rows_all - LONG) // SHORT):
                    block(LONG + SHORT * s, SHORT, lengths[1 + s], k, p)

            half_pair(k)
            cols = slice(p * 384, (p + 1) * 384)
            weight_grad(out_ref, (1 + p if k == 0 else 9 + p,), x_ref, dqkv_ref.at[k], cols)
            if k == 0:
                red.swap(9 + p)
            after[p, k]()

    bias_rows = ((b1p_ref, vsend_ref), (b1o_ref, vec_ref.at[0]))
    for k, (b1_ref, ref) in enumerate(bias_rows):
        ref[...] = jnp.zeros(ref.shape, F32)
        ref[0:3, :] = grad_ref[0:3, :]
        ref[3:6, :] = grad2_ref[0:3, :]
        ref[6:7, :] = b1_ref[0:1, 0:d]
        ref[7:8, :] = b1_ref[0:1, d:2 * d]
        sums = jnp.sum(dqkv_ref[k].astype(F32), axis=0, keepdims=True)
        ref[8:9, :] = sums[:, 0:d]
        ref[9:10, 0:sums.shape[1] - d] = sums[:, d:]
    vnow = remote(vsend_ref, vin_ref.at[BITS], vs_sem.at[BITS], vr_sem.at[BITS], red.partner)
    vnow.start()
    red.move(11)
    for copy in last:
        copy.wait()

    def back(i, _):
        rows = spans(i * tile, tile)
        dx_ref[rows, :] += dot_nt(dqkv_ref[1, rows, :], wc_ref[1]) + dot_nt(dqkv_ref[0, rows, :], wc_ref[0])
        return 0

    def vmove(step):
        vec_ref[step + 1] = vec_ref[step] + vin_ref[step]

    tiles = rows_all // tile
    outs = []
    span = rows_all // 2
    for i in range(tiles):
        lax.fori_loop(i, i + 1, back, 0)
        if i * tile % span == span - tile:
            g = i * tile // span
            here = dx_ref.at[pl.ds(g * span, span)]
            there = dx_out.at[pl.ds(pl.multiple_of((2 * g + tensor) * span, span), span)]
            outs.append(pltpu.make_async_copy(here, there, out_sem.at[g]))
            outs.append(remote(here, there, swap_sem.at[0, g], swap_sem.at[1, g], red.partner))
            outs[-1].start()
            outs[-2].start()
        if i < BITS:
            vnow.wait()
            if i == 0:
                vec_ref[0] = vec_ref[0] + vin_ref[BITS]
            else:
                vmove(i - 1)
            vnow = remote(vec_ref.at[i], vin_ref.at[i], vs_sem.at[i], vr_sem.at[i], red.links[i][1])
            vnow.start()
        if i == 0:
            red.move(10)
        if i == 1:
            red.move(8, 9, 11)
        if i == 2:
            finish(6, 7)
            red.move(10)
    red.move(11, 9)
    finish(8)
    red.move(10, 11)
    vnow.wait()
    vec_out[...] = vec_ref[BITS - 1] + vin_ref[BITS - 1]
    finish(9, 10, 11)
    for copy in outs:
        copy.wait()


def attn_back(sub, slots, sums, dh, n1, r1, gain, tokens, qkv, a, lse, wo, wc, grad2, b1):
    rows, d = dh.shape
    inner = a[0].shape[1]
    ff = b1[0].shape[1]
    units = sums.shape[0] + 1 + 3 * inner // UNIT
    shape = jax.ShapeDtypeStruct
    return pl.pallas_call(
        functools.partial(attn_back_kernel, sub),
        out_shape=(
            shape((ff, 48), F32), shape((48, ff), F32), shape((48, inner), F32), shape((48, inner), F32),
            shape((48, inner), F32), shape((inner, 48), F32), shape((2 * rows, d), F32), shape((16, d), F32),
        ),
        in_specs=[SM, SM, SM, ANY, ANY, ANY, ANY, VM] + [ANY] * 11 + [VM, VM, VM],
        out_specs=(VM, VM, VM, VM, VM, VM, ANY, VM),
        scratch_shapes=[
            pltpu.VMEM((rows, d), F32), pltpu.VMEM((rows, d), F32), pltpu.VMEM((rows, 128), F32),
            pltpu.VMEM((rows, d), BF), pltpu.VMEM((2, rows, 3 * inner), BF), pltpu.VMEM((2, rows, inner), BF),
            pltpu.VMEM((2, rows, 128), F32), pltpu.VMEM((2, inner, d), BF), pltpu.VMEM((2, d, 3 * inner), BF),
            pltpu.VMEM((rows, d), BF), pltpu.VMEM((2, rows, inner), BF), pltpu.VMEM((2, rows, 3 * inner), BF),
            pltpu.VMEM((8, d), F32), pltpu.VMEM((16, d), F32), pltpu.VMEM((BITS, 16, d), F32), pltpu.VMEM((BITS + 1, 16, d), F32),
            pltpu.VMEM((units, 2, 2, 2, 2, 48, UNIT), BF), pltpu.VMEM((4, 2, 2, 2, 2, 48, UNIT), BF),
            *halving_scratch(FIRST_B, units), pltpu.SemaphoreType.DMA((BITS + 1,)), pltpu.SemaphoreType.DMA((BITS + 1,)),
            pltpu.SemaphoreType.DMA((32,)), pltpu.SemaphoreType.DMA((2,)), pltpu.SemaphoreType.DMA((2, 2)),
        ],
        compiler_params=params(collective_id=2, has_side_effects=True),
        name="attn_back",
    )(*slots, sums, dh, n1, r1, gain, tokens, *qkv, *a, *lse, *wo, *wc, grad2, *b1)


def per_device(
    dp_size, tokens, cotangent, long_lengths, short_lengths, live_counts, query_weight, query_bias, key_weight,
    value_weight, value_bias, output_weight, output_bias, attn_gain, attn_shift, inner_weight, inner_bias,
    outer_weight, outer_bias, ffn_gain, ffn_shift,
):
    d = tokens.shape[1]
    sub = dp_size // GROUPS
    tensor = lax.axis_index("tensor")
    dp = lax.axis_index("dp")
    n_long, n_short = long_lengths.shape[0], short_lengths.shape[0]
    rows = n_long // 2 * LONG
    pairs = query_weight.shape[1] // PAIR
    slots = (long_lengths, short_lengths, live_counts)

    def both(own, other):
        return jnp.where(tensor == 0, own, other), jnp.where(tensor == 0, other, own)

    def swap(a):
        return lax.ppermute(a, "tensor", [(0, 1), (1, 0)])

    bias_own = jnp.concatenate([query_bias, value_bias, inner_bias]).reshape(1, -1)
    weights = (query_weight, key_weight, value_weight)
    weights_other = tuple(swap(w) for w in weights)
    bias_other = swap(bias_own)
    wo_other, w1_other, w2_other = swap(output_weight), swap(inner_weight), swap(outer_weight)

    qkv_own, a_own, lse_own, wc_own = attend(slots, tokens, weights, bias_own)
    qkv_other, a_other, lse_other, wc_other = attend(slots, tokens, weights_other, bias_other)
    vectors = [a.reshape(1, d) for a in (output_bias, attn_gain, attn_shift, outer_bias, ffn_gain, ffn_shift)]
    (result, pooled, n1, r1, h, g_own, g_other, slope_own, slope_other, df, dr, grad2) = forward(
        slots, tokens, cotangent, a_own, a_other, (output_weight, wo_other), (inner_weight, w1_other),
        (outer_weight, w2_other), (bias_own, bias_other), vectors)
    result_other = swap(result)
    pooled_own = jnp.concatenate([pooled[:n_long // 2], pooled[8:8 + n_short // 2]])
    pooled_other = swap(pooled_own)
    sums, dh, b1p, b1o = ffn_back(
        sub, df, h, dr, (g_other, g_own), (slope_other, slope_own), (w1_other, inner_weight), (w2_other, outer_weight))
    d_outer, d_inner, d_q, d_k, d_v, d_output, dx, total = attn_back(
        sub, slots, sums, dh, n1, r1, vectors[1], tokens, (qkv_other, qkv_own), (a_other, a_own),
        (lse_other, lse_own), (wo_other, output_weight), (wc_other, wc_own), grad2, (b1p, b1o))

    if sub > 1:
        groups = [[g * sub + i for i in range(sub)] for g in range(GROUPS)]

        def rest(a, dim):
            return lax.psum_scatter(a, "dp", scatter_dimension=dim, axis_index_groups=groups, tiled=True)

        d_outer, d_output = rest(d_outer, 1), rest(d_output, 1)
        d_inner, d_q, d_k, d_v = (rest(a, 0) for a in (d_inner, d_q, d_k, d_v))
        total = lax.psum(total, "dp", axis_index_groups=groups)
    mine_of = lax.dynamic_slice_in_dim(total, dp * (d // dp_size), d // dp_size, 1)
    d_b1 = total[6:8].reshape(-1)
    d_bc = total[8:10].reshape(-1)[:pairs * 384].reshape(pairs, 3, PAIR)

    first, second = both(result, result_other)
    result_all = jnp.concatenate([first[:rows], second[:rows], first[rows:], second[rows:]], axis=0)
    pooled_both = both(pooled_own, pooled_other)
    pooled_all = jnp.concatenate(
        [p[:n_long // 2] for p in pooled_both] + [p[n_long // 2:] for p in pooled_both])
    return (
        result_all, pooled_all, dx, d_q, d_bc[:, 0].reshape(-1), d_k, d_v, d_bc[:, 2].reshape(-1), d_output,
        mine_of[0], mine_of[1], mine_of[2], d_inner, d_b1, d_outer, mine_of[3], mine_of[4], mine_of[5],
    )


def solution(mesh):
    in_specs = (
        P("dp", None), P("dp", None), P("dp"), P("dp"), P("dp", None), P(None, "tensor"), P("tensor"),
        P(None, "tensor"), P(None, "tensor"), P("tensor"), P("tensor", None), P(), P(), P(), P(None, "tensor"),
        P("tensor"), P("tensor", None), P(), P(), P(),
    )
    out_specs = (
        P("dp", None), P("dp", None), P("dp", None), P("dp", "tensor"), P("tensor"), P("dp", "tensor"),
        P("dp", "tensor"), P("tensor"), P("tensor", "dp"), P("dp"), P("dp"), P("dp"), P("dp", "tensor"),
        P("tensor"), P("tensor", "dp"), P("dp"), P("dp"), P("dp"),
    )
    return jax.shard_map(
        functools.partial(per_device, mesh.shape["dp"]), mesh=mesh, in_specs=in_specs, out_specs=out_specs,
        check_vma=False)
```

time: 1170 us -> 219 us (0.19)
  waiting for transfers between devices: 756 us -> 2.39 us
  matrix products: 197 us -> 0 us
  Pallas kernels: 0 us -> 180 us
  blocking collectives: 77.2 us -> 0 us
  other arithmetic: 56.2 us -> 3.44 us
  local copies, waits for them, and re-layouts: 67.8 us -> 26.1 us
  between operations: 15.9 us -> 1.16 us
    unnamed x13 -> x0, waiting for transfers between devices: 384 us -> none
    reduce_scatter x3 -> x0, waiting for transfers between devices: 297 us -> none  [the longest x1 143 us: per_device(): lax.psum_scatter(inner_weight_grad, 'dp', scatter_dimension=0, tiled=True)]
    dot_general x29 -> x0, matrix products: 186 us -> none  [the longest x2 28.3 us: attend_back(): jnp.einsum('bhqk,bqhd->bkhd', score_grad, queries, preferred_element_type...]
    pallas_call x0 -> x5, Pallas kernels: none -> 180 us  [the longest x1 71.6 us: attn_back(): pl.pallas_call(functools.partial(attn_back_kernel, sub), out_shape=(shape...]
    psum x1 -> x0, blocking collectives: 77.2 us -> none  [per_device(): lax.psum((query_bias_grad, value_bias_grad, inner_bias_grad), 'dp')]
    psum x4 -> x0, waiting for transfers between devices: 75 us -> none  [the longest x1 26 us: per_device(): lax.psum(jnp.dot(heads_low, output_weight, preferred_element_type=jnp.flo...]
    reduce_sum x11 -> x0, other arithmetic: 36.3 us -> none  [the longest x2 15.5 us: normalize_back(): jnp.sum(upstream * normed, axis=0)]
    slice x14 -> x10, local copies, waits for them, and re-layouts: 22.7 us -> 3.08 us  [the longest x1 0.76 us: per_device(): d_b1 = total[6:8].reshape(-1)]
  transfers between devices with their start and end apart: 10 -> 9, of which waited for: 9 -> 1; matrix products, arithmetic and copies ran while one was open for 5% -> 8% of each run, Pallas kernels for 0% -> 67%
where the time goes in v1:
time: 219 us; the launch traced here: 216 us
  Pallas kernels  180 us (82%)
  local copies, waits for them, and re-layouts  26.1 us (12%)
  other arithmetic  3.44 us (2%)
  starting transfers between devices  2.6 us (1%)
  waiting for transfers between devices  2.39 us (1%)
    pallas_call x1, Pallas kernels, attn_back(): pl.pallas_call(functools.partial(attn_back_kernel, sub), out_shape=(shape...  71.6 us
    pallas_call x1, Pallas kernels, ffn_back(): pl.pallas_call(functools.partial(ffn_back_kernel, sub), out_shape=(shape(...  44.2 us
    pallas_call x1, Pallas kernels, forward(): pl.pallas_call(forward_kernel, grid=(2,), out_shape=(shape((rows, d), BF)...  34.5 us
    pallas_call x2, Pallas kernels, attend(): pl.pallas_call(attend_kernel, out_shape=(shape((rows, 3 * inner), BF), sh...  29.5 us
    unnamed x33, local copies, waits for them, and re-layouts  13.2 us
    reshape x6, local copies, waits for them, and re-layouts, per_device(): a.reshape(1, d)  7.62 us
  transfers between devices with their start and end apart: 9, of which 1 were waited for; matrix products, arithmetic and copies ran while one was open for 8% of the time, Pallas kernels for 67%

profile of v1, /device:TPU:0, one launch (start us, length us, event | category | flops | bytes accessed | tf_op | source)
XLA Modules:
  0.0 215.5 jit_solution(3630161216183884263)
XLA Ops:
  0.7 0.5 collective-permute-start.5
  1.2 0.1 collective-permute-start.6
  1.3 0.4 collective-permute-start
  1.7 0.7 pad_maximum_fusion.3
  2.4 0.0 copy-start.8
  2.4 0.1 collective-permute-start.3
  2.6 0.4 collective-permute-start.1
  3.0 2.4 %collective-permute-done.3.bias_ref.bp_ref = f32[1,2304]{1,0:T(1,128)S(1)} collective-permute-done((f32[1,2304]{1,0:T(1,128)S(1)}, f32[1,2304]{1,0:T(1,128)S(1)}, u32[]{:S(2)}, u32[]{:S(2)}) %collective-permute-start.3) | collective-permute-done | bytes 9248 | tf_op jit(solution)/shard_map/ppermute | solution.py:803
  5.4 0.4 collective-permute-start.2
  5.7 1.3 reshape.66.a1_ref.gain_ref
  7.0 1.3 reshape.65.attn_bias_ref
  8.3 1.3 reshape.67.s1_ref
  9.6 1.3 reshape.68.ffn_bias_ref
  10.8 1.3 reshape.69.a2_ref
  12.1 1.3 reshape.70.s2_ref
  13.4 0.0 collective-permute-done.wq_ref
  13.4 0.1 collective-permute-start.4
  13.5 15.0 %attend.2 = (bf16[1024,1152]{1,0:T(8,128)(2,1)}, bf16[1024,384]{1,0:T(8,128)(2,1)}, f32[1024,128]{1,0:T(8,128)}, bf16[768,1152]{1,0:T(8,128)(2,1)}) custom-call(s32[2]{0:T(128)} %long_ref.7, s32[8]{0:T(128)} %short_ref.7, s32[1,2]{1,0:T(1,128)} %count_ref.7, bf16[2048,768]{1,0:T(8,128)(2,1)} %tok_hbm.1, bf16[768,384]{1,0:T(8,128)(2,1)} %wq_ref.1, ...), custom_call_target="tpu_custom_call" | custom-call | flops 3422552064 | bytes 8388608 | tf_op jit(solution)/shard_map/attend/pallas_call | solution.py:144
  28.5 0.0 collective-permute-done.1.wk_ref
  28.5 0.0 collective-permute-done.2.wv_ref
  28.6 14.5 %attend.3 = (bf16[1024,1152]{1,0:T(8,128)(2,1)}, bf16[1024,384]{1,0:T(8,128)(2,1)}, f32[1024,128]{1,0:T(8,128)}, bf16[768,1152]{1,0:T(8,128)(2,1)}) custom-call(s32[2]{0:T(128)} %long_ref.7, s32[8]{0:T(128)} %short_ref.7, s32[1,2]{1,0:T(1,128)} %count_ref.7, bf16[2048,768]{1,0:T(8,128)(2,1)} %tok_hbm.1, bf16[768,384]{1,0:T(8,128)(2,1)} %copy-done.9, ...), custom_call_target="tpu_custom_call" | custom-call | flops 3422552064 | bytes 8388608 | tf_op jit(solution)/shard_map/attend/pallas_call | solution.py:144
  43.2 0.8 copy-done.3
  44.0 0.8 copy-done
  44.8 0.7 copy-done.1
  45.5 34.5 %forward.1 = (bf16[1024,768]{1,0:T(8,128)(2,1)}, f32[16,768]{1,0:T(8,128)}, f32[1024,768]{1,0:T(8,128)}, f32[1024,128]{1,0:T(8,128)}, bf16[1024,768]{1,0:T(8,128...) custom-call(s32[2]{0:T(128)} %long_ref.7, ...), custom_call_target="tpu_custom_call" | custom-call | flops 10871635968 | bytes 52428800 | tf_op jit(solution)/shard_map/forward/pallas_call | solution.py:305
  80.0 0.4 collective-permute-start.7
  80.5 0.7 slice.71
  81.2 0.7 slice.70
  81.9 44.2 %ffn_back.1 = (bf16[8,2,2,2,2,48,384]{6,5,4,3,2,1,0:T(8,128)(2,1)}, f32[1024,768]{1,0:T(8,128)}, f32[8,1536]{1,0:T(8,128)}, f32[8,1536]{1,0:T(8,128)}) custom-call(bf16[1024,768]{1,0:T(8,128)(2,1)} %get-tuple-element.54.df_hbm, bf16[1024,768]{1,0:T(8,128)(2,1)} %get-tuple-element.55.h_hbm, f32[1024,768]{1,0:T(8,128)} %get-tuple-element.56.dr_hbm, ...), custom_call_target="tpu_custom_call" | custom-call | tf_op jit(solution)/shard_map/ffn_back/pallas_call | solution.py:527
  126.1 71.6 %attn_back.1 = (f32[1536,48]{1,0:T(8,128)}, f32[48,1536]{1,0:T(8,128)}, f32[48,384]{1,0:T(8,128)}, f32[48,384]{1,0:T(8,128)}, f32[48,384]{1,0:T(8,128)}, /*index...) custom-call(s32[2]{0:T(128)} %long_ref.7, s32[8]{0:T(128)} %short_ref.7, s32[1,2]{1,0:T(1,128)} %count_ref.7, ...), custom_call_target="tpu_custom_call" | custom-call | tf_op jit(solution)/shard_map/attn_back/pallas_call | solution.py:762
  197.8 0.8 fusion.2
  198.6 0.1 collective-permute-start.8
  198.6 0.6 slice_reduce_fusion
  199.3 1.5 dynamic-slice_bitcast_fusion
  200.8 2.1 copy.41
  202.9 1.7 copy.40
  204.5 0.6 reshape.71
  205.2 0.6 pad_maximum_fusion.1
  205.9 0.2 broadcast_select_fusion.1
  206.1 0.2 fusion
  206.3 1.8 pad_maximum_fusion
  208.1 1.0 slice-done
  209.2 0.7 slice-done.1
  209.9 2.7 %copy.47 = f32[2048,768]{1,0:T(8,128)} copy(f32[2048,768]{1,0:T(8,128)S(1)} %bitcast.15) | data formatting | bytes 12582912
  212.6 0.6 copy.48
  213.3 0.6 copy.49
  213.9 0.6 copy.50
  214.6 0.7 copy.51
  (34 shorter events, 0.1 us)
Async XLA Ops:
  0.7 42.5 %collective-permute-start.5 = (bf16[768,1536]{1,0:T(8,128)(2,1)}, bf16[768,1536]{1,0:T(8,128)(2,1)S(1)}, u32[]{:S(2)}, u32[]{:S(2)}) collective-permute-start(bf16[768,1536]{1,0:T(8,128)(2,1)} %w1o_hbm.3), channel_id=1, source_target_pairs={{0,1},{1,0},{2,3},{3,2},{4,5},{5,4},{6,7},{7,6},{8,9},{9,8},{10,11... | collective-permute-start | bytes 7077896 | tf_op jit(solution)/shard_map/ppermute | solution.py:803
  1.2 42.0 %collective-permute-start.6 = (bf16[1536,768]{1,0:T(8,128)(2,1)}, bf16[1536,768]{1,0:T(8,128)(2,1)S(1)}, u32[]{:S(2)}, u32[]{:S(2)}) collective-permute-start(bf16[1536,768]{1,0:T(8,128)(2,1)} %w2o_hbm.3), channel_id=1, source_target_pairs={{0,1},{1,0},{2,3},{3,2},{4,5},{5,4},{6,7},{7,6},{8,9},{9,8},{10,11... | collective-permute-start | bytes 7077896 | tf_op jit(solution)/shard_map/ppermute | solution.py:803
  1.3 12.1 %collective-permute-start = (bf16[768,384]{1,0:T(8,128)(2,1)}, bf16[768,384]{1,0:T(8,128)(2,1)S(1)}, u32[]{:S(2)}, u32[]{:S(2)}) collective-permute-start(bf16[768,384]{1,0:T(8,128)(2,1)} %wq_ref.1), channel_id=1, source_target_pairs={{0,1},{1,0},{2,3},{3,2},{4,5},{5,4},{6,7},{7,6},{8,9},{9,8},{10,11... | collective-permute-start | bytes 1769480 | tf_op jit(solution)/shard_map/ppermute | solution.py:803
  2.4 11.1 %copy-start.8 = (f32[1,2304]{1,0:T(1,128)}, f32[1,2304]{1,0:T(1,128)S(1)}, u32[]{:S(2)}) copy-start(f32[1,2304]{1,0:T(1,128)S(1)} %reshape.64.bias_ref.bo_ref) | copy-start | bytes 27652
  2.4 2.9 %collective-permute-start.3 = (f32[1,2304]{1,0:T(1,128)S(1)}, f32[1,2304]{1,0:T(1,128)S(1)}, u32[]{:S(2)}, u32[]{:S(2)}) collective-permute-start(f32[1,2304]{1,0:T(1,128)S(1)} %reshape.64.bias_ref.bo_ref), channel_id=1, source_target_pairs={{0,1},{1,0},{2,3},{3,2},{4,5},{5,4},{6,7},{7,6},{8,9},{9,8},{10,11... | collective-permute-start | bytes 27656 | tf_op jit(solution)/shard_map/ppermute | solution.py:803
  2.6 26.0 %collective-permute-start.1 = (bf16[768,384]{1,0:T(8,128)(2,1)}, bf16[768,384]{1,0:T(8,128)(2,1)}, u32[]{:S(2)}, u32[]{:S(2)}) collective-permute-start(bf16[768,384]{1,0:T(8,128)(2,1)} %wk_ref.1), channel_id=1, source_target_pairs={{0,1},{1,0},{2,3},{3,2},{4,5},{5,4},{6,7},{7,6},{8,9},{9,8},{10,11... | collective-permute-start | bytes 1769480 | tf_op jit(solution)/shard_map/ppermute | solution.py:803
  5.4 23.1 %copy-start.10 = (f32[1,2304]{1,0:T(1,128)}, f32[1,2304]{1,0:T(1,128)S(1)}, u32[]{:S(2)}) copy-start(f32[1,2304]{1,0:T(1,128)S(1)} %collective-permute-done.3.bias_ref.bp_ref) | copy-start | bytes 27652
  5.4 23.2 %collective-permute-start.2 = (bf16[768,384]{1,0:T(8,128)(2,1)}, bf16[768,384]{1,0:T(8,128)(2,1)}, u32[]{:S(2)}, u32[]{:S(2)}) collective-permute-start(bf16[768,384]{1,0:T(8,128)(2,1)} %wv_ref.1), channel_id=1, source_target_pairs={{0,1},{1,0},{2,3},{3,2},{4,5},{5,4},{6,7},{7,6},{8,9},{9,8},{10,11... | collective-permute-start | bytes 1769480 | tf_op jit(solution)/shard_map/ppermute | solution.py:803
  13.4 15.2 %copy-start.9 = (bf16[768,384]{1,0:T(8,128)(2,1)}, bf16[768,384]{1,0:T(8,128)(2,1)S(1)}, u32[]{:S(2)}) copy-start(bf16[768,384]{1,0:T(8,128)(2,1)S(1)} %collective-permute-done.wq_ref) | copy-start | bytes 1769476
  13.4 29.7 %collective-permute-start.4 = (bf16[384,768]{1,0:T(8,128)(2,1)}, bf16[384,768]{1,0:T(8,128)(2,1)S(1)}, u32[]{:S(2)}, u32[]{:S(2)}) collective-permute-start(bf16[384,768]{1,0:T(8,128)(2,1)} %woo_hbm.1), channel_id=1, source_target_pairs={{0,1},{1,0},{2,3},{3,2},{4,5},{5,4},{6,7},{7,6},{8,9},{9,8},{10,11... | collective-permute-start | bytes 1769480 | tf_op jit(solution)/shard_map/ppermute | solution.py:803
  43.1 0.8 copy-start.3
  43.1 1.6 copy-start
  43.2 2.4 %copy-start.1 = (bf16[1536,768]{1,0:T(8,128)(2,1)}, bf16[1536,768]{1,0:T(8,128)(2,1)S(1)}, u32[]{:S(2)}) copy-start(bf16[1536,768]{1,0:T(8,128)(2,1)S(1)} %collective-permute-done.6.w2p_hbm) | copy-start | bytes 7077892
  80.0 125.8 %collective-permute-start.7 = (bf16[1024,768]{1,0:T(8,128)(2,1)}, bf16[1024,768]{1,0:T(8,128)(2,1)S(1)}, u32[]{:S(2)}, u32[]{:S(2)}) collective-permute-start(bf16[1024,768]{1,0:T(8,128)(2,1)} %get-tuple-element.52), channel_id=1, source_target_pairs={{0,1},{1,0},{2,3},{3,2},{4,5},{5,4},{6,7},{7,6},{8,9},{9,8},{10,11... | collective-permute-start | bytes 4718600 | tf_op jit(solution)/shard_map/ppermute | solution.py:803
  126.1 79.7 %copy-start.2 = (bf16[1024,768]{1,0:T(8,128)(2,1)S(1)}, bf16[1024,768]{1,0:T(8,128)(2,1)}, u32[]{:S(2)}) copy-start(bf16[1024,768]{1,0:T(8,128)(2,1)} %get-tuple-element.52) | copy-start | bytes 4718596
  198.6 6.6 %collective-permute-start.8 = (f32[5,768]{1,0:T(8,128)S(1)}, f32[5,768]{1,0:T(8,128)S(1)}, u32[]{:S(2)}, u32[]{:S(2)}) collective-permute-start(f32[5,768]{1,0:T(8,128)S(1)} %pad_maximum_fusion.2), channel_id=1, source_target_pairs={{0,1},{1,0},{2,3},{3,2},{4,5},{5,4},{6,7},{7,6},{8,9},{9,8},{10,11... | collective-permute-start | bytes 46088 | tf_op jit(solution)/shard_map/ppermute | solution.py:803
  205.9 3.3 %slice-start = ((s8[6291456]{0:T(1024)(128)(4,1)}), s8[4194304]{0:T(1024)(128)(4,1)S(1)}, s32[]{:S(2)}) async-start(s8[6291456]{0:T(1024)(128)(4,1)} %bitcast.14), calls=%async_computation | async-start | bytes 8388608
  206.1 3.8 %slice-start.1 = ((s8[6291456]{0:T(1024)(128)(4,1)}), s8[2097152]{0:T(1024)(128)(4,1)S(1)}, s32[]{:S(2)}) async-start(s8[6291456]{0:T(1024)(128)(4,1)} %bitcast.14), calls=%async_computation.1 | async-start | bytes 4194304
  209.9 2.7 %copy-start.7 = (f32[48,384]{1,0:T(8,128)S(1)}, f32[48,384]{1,0:T(8,128)}, u32[]{:S(2)}) copy-start(f32[48,384]{1,0:T(8,128)} %get-tuple-element.159) | copy-start | bytes 221188
  209.9 3.4 %copy-start.6 = (f32[48,384]{1,0:T(8,128)S(1)}, f32[48,384]{1,0:T(8,128)}, u32[]{:S(2)}) copy-start(f32[48,384]{1,0:T(8,128)} %get-tuple-element.161) | copy-start | bytes 221188
  209.9 4.0 %copy-start.5 = (f32[48,384]{1,0:T(8,128)S(1)}, f32[48,384]{1,0:T(8,128)}, u32[]{:S(2)}) copy-start(f32[48,384]{1,0:T(8,128)} %get-tuple-element.162) | copy-start | bytes 221188
  209.9 4.6 %copy-start.4 = (f32[48,1536]{1,0:T(8,128)S(1)}, f32[48,1536]{1,0:T(8,128)}, u32[]{:S(2)}) copy-start(f32[48,1536]{1,0:T(8,128)} %get-tuple-element.168) | copy-start | bytes 884740
